TPU v7x, 32 devices: a whole 2x2x4 slice. The times are simulated.
32 devices in a mesh: shard: 8 (over z, core), batch: 4 (over y, x).
Axes of the slice: x: 2, y: 2, z: 4, core: 2. Of those that a mesh axis runs over, the one named last changes fastest.
Arguments:
- data_inputs: bfloat16 [8, 256, 1024], P('shard', 'batch'), may hold values from -6 to 6
- data_targets: bfloat16 [8, 256, 512], P('shard', 'batch'), may hold values from -6 to 6
- row_picks: int32 [2, 8, 512], P(None, 'shard', 'batch'), may hold values from 0 to 63
- layer_one: float32 [8, 1024, 2048], P('shard', None, 'batch'), may hold values from -6 to 6
- layer_two: float32 [8, 2048, 512], P('shard', 'batch'), may hold values from -6 to 6
- noise_one: bfloat16 [2, 8, 1024, 2048], P(None, 'shard', None, 'batch'), may hold values from -6 to 6
- noise_two: bfloat16 [2, 8, 2048, 512], P(None, 'shard', 'batch'), may hold values from -6 to 6
Outputs:
- moved_one: float32 [8, 1024, 2048], P('shard', None, 'batch')
- moved_two: float32 [8, 2048, 512], P('shard', 'batch')
- last_errors: bfloat16 [8, 512, 512], P('shard', 'batch')
All inputs are finite; a program needn't handle non-finite values.
Results may differ from a plain program's by a relative error of at most 0.014.
Values may be sent and summed in bfloat16 or wider, within the bound.
A program may use at most 64 MiB of HBM per device.

v0:
```python
import jax
import jax.numpy as jnp
from jax import lax
from jax.sharding import PartitionSpec as P

D_IN = 1024
HID = 2048
STEPS = 2
half_step = 0.01
root_step = 0.02**0.5
precision_obs = 32.0


def passed_along(value, axis, by):
    size = lax.axis_size(axis)
    return lax.ppermute(value, axis, [(i, (i + by) % size) for i in range(size)])


def per_device(data_inputs, data_targets, row_picks, layer_one, layer_two, noise_one, noise_two):
    scale_in = D_IN ** (-0.5)
    scale_hid = HID ** (-0.5)
    weights_a = layer_one[0]
    weights_b = layer_two[0]
    contract_rows = (((0,), (0,)), ((), ()))
    contract_cols = (((1,), (1,)), ((), ()))
    own_errors = jnp.zeros((row_picks.shape[2], weights_b.shape[1]), jnp.float32)
    for iteration in range(STEPS):
        chosen = row_picks[iteration, 0]
        local_rows = jnp.take(data_inputs[0], chosen, axis=0)
        local_targets = jnp.take(data_targets[0], chosen, axis=0)
        bf_a = weights_a.astype(jnp.bfloat16)
        bf_b = weights_b.astype(jnp.bfloat16)
        all_rows = lax.all_gather(local_rows, "batch", axis=0, tiled=True)
        hidden = jnp.tanh(jnp.dot(all_rows, bf_a, preferred_element_type=jnp.float32) * scale_in)
        hidden_b = hidden.astype(jnp.bfloat16)
        predicted = lax.psum_scatter(
            (jnp.dot(hidden_b, bf_b, preferred_element_type=jnp.float32) * scale_hid).astype(
                jnp.bfloat16
            ),
            "batch",
            scatter_dimension=0,
            tiled=True,
        ).astype(jnp.float32)
        own_errors = predicted - local_targets.astype(jnp.float32)
        signal = lax.all_gather(
            (precision_obs * own_errors).astype(jnp.bfloat16), "batch", axis=0, tiled=True
        )
        grad_two = (
            lax.dot_general(hidden_b, signal, contract_rows, preferred_element_type=jnp.float32)
            * scale_hid
        )
        back_hidden = (
            lax.dot_general(signal, bf_b, contract_cols, preferred_element_type=jnp.float32)
            * scale_hid
            * (1.0 - hidden * hidden)
        ).astype(jnp.bfloat16)
        grad_one = (
            lax.dot_general(
                all_rows, back_hidden, contract_rows, preferred_element_type=jnp.float32
            )
            * scale_in
        )
        weights_a = (
            weights_a
            - half_step * (grad_one + weights_a)
            + root_step * noise_one[iteration, 0].astype(jnp.float32)
        )
        weights_b = (
            weights_b
            - half_step * (grad_two + weights_b)
            + root_step * noise_two[iteration, 0].astype(jnp.float32)
        )
    moved_a, moved_b = (
        passed_along(weights_a.astype(jnp.bfloat16), "shard", 1).astype(weights_a.dtype),
        passed_along(weights_b.astype(jnp.bfloat16), "shard", 1).astype(weights_b.dtype),
    )
    return (moved_a[None], moved_b[None], own_errors.astype(jnp.bfloat16)[None])


def solution(mesh):
    in_specs = (
        P("shard", "batch", None),
        P("shard", "batch", None),
        P(None, "shard", "batch"),
        P("shard", None, "batch"),
        P("shard", "batch", None),
        P(None, "shard", None, "batch"),
        P(None, "shard", "batch", None),
    )
    out_specs = (P("shard", None, "batch"), P("shard", "batch", None), P("shard", "batch", None))
    return jax.shard_map(
        per_device, mesh=mesh, in_specs=in_specs, out_specs=out_specs, check_vma=False
    )
```

profile of v0, /device:TPU:0, one launch (start us, length us, event | category | flops | bytes accessed | tf_op | source)
XLA Modules:
  0.0 173.4 jit_solution(172406984584624309)
XLA Ops:
  7.2 0.0 copy-start
  7.2 0.0 all-gather.3.cloned.1.call-start
  7.2 0.7 compare_and_fusion
  7.9 0.1 copy-done
  8.1 0.9 gather_fusion
  8.9 0.8 broadcast_select_fusion.1
  9.7 0.0 all-gather.3.cloned.1.call-update
  9.8 0.0 copy-start.2
  9.8 0.0 reduce-scatter.3.cloned.1.call-start
  9.8 30.0 %all-gather.3.cloned.1.call-done = bf16[512,1024]{1,0:T(8,128)(2,1)} async-done(((bf16[128,1024]{1,0:T(8,128)(2,1)}), bf16[512,1024]{1,0:T(8,128)(2,1)}) %all-gather.3.cloned.1.call-update) | async-done | bytes 1048592 | tf_op jit(solution)/shard_map/all_gather | solution.py:33
  39.8 2.6 %fusion.13 = f32[512,512]{1,0:T(8,128)S(1)} fusion(bf16[512,1024]{1,0:T(8,128)(2,1)} %all-gather.3.cloned.1.call-done, f32[1,1024,512]{2,1,0:T(8,128)} %param.14), kind=kOutput, calls=%fused_computation.30 | convolution fusion | flops 537133056 | bytes 4194304 | tf_op jit(solution)/shard_map/dot_general | solution.py:34
  42.4 0.0 copy-done.2
  42.4 1.2 fusion.17
  43.7 0.0 copy-start.1
  43.7 0.0 reduce-scatter.3.cloned.1.call-update
  43.7 0.0 all-gather.5.cloned.1.call-start
  43.8 0.9 gather_fusion.2
  44.6 0.8 broadcast_select_fusion
  45.4 0.0 all-gather.5.cloned.1.call-update
  45.5 0.0 reduce-scatter.5.cloned.1.call-start
  45.5 0.0 copy-done.1
  45.5 0.8 gather_fusion.1
  46.4 22.3 %reduce-scatter.3.cloned.1.call-done = bf16[128,512]{1,0:T(8,128)(2,1)} async-done(((bf16[512,512]{1,0:T(8,128)(2,1)}), bf16[128,512]{1,0:T(8,128)(2,1)}) %reduce-scatter.3.cloned.1.call-update) | async-done | bytes 131088 | tf_op jit(solution)/shard_map/reduce_scatter | solution.py:36
  68.6 1.0 multiply_convert_fusion.1
  69.7 10.0 %all_gather.13 = bf16[512,512]{1,0:T(8,128)(2,1)S(1)} all-gather(bf16[128,512]{1,0:T(8,128)(2,1)S(1)} %multiply_convert_fusion.1), channel_id=1, replica_groups=mesh['shard'=8,'batch'=4] {'batch'}, dimensions={0}, use_global_device_ids=true | all-gather | bytes 655360 | tf_op jit(solution)/shard_map/all_gather | solution.py:45
  79.7 0.0 copy-start.3
  79.7 0.8 copy-done.3
  80.5 1.6 fusion.10
  82.1 5.0 %bitcast_add_fusion.1 = f32[1024,512]{1,0:T(8,128)} fusion(f32[1,1024,512]{2,1,0:T(8,128)} %param.14, bf16[512,1024]{1,0:T(8,128)(2,1)} %all-gather.3.cloned.1.call-done, bf16[512,512]{1,0:T(8,128)(2,1)} %copy-done.3, bf16[2,1,1024,512]{3,2,1,0:T(8,128)(2,1)} %param.16, f32[512,512]{1,0:T(8,128)S(1)} %fusion.13, f32[1,512,512]{2,1,0:T(8,128)S(1)} %copy-done.2), kind=kOutput, calls=%fused_computation.6 | convolution fusion | flops 810287104 | bytes 8912896 | tf_op jit(solution)/shard_map/dot_general | solution.py:58
  87.1 10.2 %all-gather.5.cloned.1.call-done = bf16[512,1024]{1,0:T(8,128)(2,1)} async-done(((bf16[128,1024]{1,0:T(8,128)(2,1)}), bf16[512,1024]{1,0:T(8,128)(2,1)}) %all-gather.5.cloned.1.call-update) | async-done | bytes 1048592 | tf_op jit(solution)/shard_map/all_gather | solution.py:33
  97.3 2.6 %fusion.11 = f32[512,512]{1,0:T(8,128)S(1)} fusion(bf16[512,1024]{1,0:T(8,128)(2,1)} %all-gather.5.cloned.1.call-done, f32[1024,512]{1,0:T(8,128)} %bitcast_add_fusion.1), kind=kOutput, calls=%fused_computation.25 | convolution fusion | flops 537657344 | bytes 4194304 | tf_op jit(solution)/shard_map/dot_general | solution.py:34
  99.9 1.2 fusion.18
  101.2 0.0 reduce-scatter.5.cloned.1.call-update
  101.2 0.8 gather_fusion.3
  102.1 24.1 %reduce-scatter.5.cloned.1.call-done = bf16[128,512]{1,0:T(8,128)(2,1)} async-done(((bf16[512,512]{1,0:T(8,128)(2,1)}), bf16[128,512]{1,0:T(8,128)(2,1)}) %reduce-scatter.5.cloned.1.call-update) | async-done | bytes 131088 | tf_op jit(solution)/shard_map/reduce_scatter | solution.py:36
  126.2 1.7 fusion.36
  127.8 9.9 %all_gather.15 = bf16[512,512]{1,0:T(8,128)(2,1)S(1)} all-gather(bf16[128,512]{1,0:T(8,128)(2,1)S(1)} %get-tuple-element.10), channel_id=1, replica_groups=mesh['shard'=8,'batch'=4] {'batch'}, dimensions={0}, use_global_device_ids=true | all-gather | bytes 655360 | tf_op jit(solution)/shard_map/all_gather | solution.py:45
  137.8 4.5 %fusion = bf16[1024,512]{1,0:T(8,128)(2,1)} fusion(f32[1024,512]{1,0:T(8,128)} %bitcast_add_fusion.1, bf16[512,1024]{1,0:T(8,128)(2,1)} %all-gather.5.cloned.1.call-done, bf16[512,512]{1,0:T(8,128)(2,1)S(1)} %all_gather.15, bf16[2,1,1024,512]{3,2,1,0:T(8,128)(2,1)} %param.16, f32[512,512]{1,0:T(8,128)S(1)} %fusion.11, f32[512,512]{1,0:T(8,128)S(1)} %fusion.10), kind=kOutput, calls=%fused_computation.5 | convolution fusion | flops 811073536 | bytes 7864320 | tf_op jit(solution)/shard_map/dot_general | solution.py:58
  142.3 0.0 collective-permute-start
  142.3 1.6 fusion.16
  144.0 1.7 collective-permute-start.1
  145.6 18.6 %collective-permute-done.1 = bf16[512,512]{1,0:T(8,128)(2,1)S(1)} collective-permute-done((bf16[512,512]{1,0:T(8,128)(2,1)S(1)}, bf16[512,512]{1,0:T(8,128)(2,1)S(1)}, u32[]{:S(2)}, u32[]{:S(2)}) %collective-permute-start.1) | collective-permute-done | bytes 524320 | tf_op jit(solution)/shard_map/ppermute | solution.py:16
  164.2 1.1 bitcast_convert_fusion.4
  165.3 0.0 collective-permute-done
  165.3 1.6 bitcast_convert_fusion.2
  (2 shorter events, 0.0 us)
Async XLA Ops:
  7.2 0.9 copy-start
  7.2 32.6 %all-gather.3.cloned.1.call-start = ((), (), s32[]{:S(2)}) async-start(), calls=%async_computation.2 | async-start | bytes 1310720 | tf_op jit(solution)/shard_map/all_gather | solution.py:33
  9.8 32.7 %copy-start.2 = (f32[1,512,512]{2,1,0:T(8,128)S(1)}, f32[1,512,512]{2,1,0:T(8,128)}, u32[]{:S(2)}) copy-start(f32[1,512,512]{2,1,0:T(8,128)} %param.15) | copy-start | bytes 3145732
  9.8 58.9 %reduce-scatter.3.cloned.1.call-start = ((), (), s32[]{:S(2)}) async-start(), calls=%async_computation.3 | async-start | bytes 655360 | tf_op jit(solution)/shard_map/reduce_scatter | solution.py:36
  43.7 1.8 %copy-start.1 = (bf16[1,64,512]{2,1,0:T(8,128)(2,1)S(1)}, bf16[1,64,512]{2,1,0:T(8,128)(2,1)}, u32[]{:S(2)}) copy-start(bf16[1,64,512]{2,1,0:T(8,128)(2,1)} %param.12) | copy-start | bytes 196612
  43.7 53.6 %all-gather.5.cloned.1.call-start = ((), (), s32[]{:S(2)}) async-start(), calls=%async_computation.4 | async-start | bytes 1310720 | tf_op jit(solution)/shard_map/all_gather | solution.py:33
  45.5 80.7 %reduce-scatter.5.cloned.1.call-start = ((), (), s32[]{:S(2)}) async-start(), calls=%async_computation.5 | async-start | bytes 655360 | tf_op jit(solution)/shard_map/reduce_scatter | solution.py:36
  79.7 0.8 copy-start.3
  142.3 23.0 %collective-permute-start = (bf16[1024,512]{1,0:T(8,128)(2,1)}, bf16[1024,512]{1,0:T(8,128)(2,1)S(1)}, u32[]{:S(2)}, u32[]{:S(2)}) collective-permute-start(bf16[1024,512]{1,0:T(8,128)(2,1)} %fusion), channel_id=1, source_target_pairs={{0,4},{4,8},{8,12},{12,16},{16,20},{20,24},{24,28},{28,0},{1,5},{5... | collective-permute-start | bytes 3145736 | tf_op jit(solution)/shard_map/ppermute | solution.py:16
  144.0 20.2 %collective-permute-start.1 = (bf16[512,512]{1,0:T(8,128)(2,1)S(1)}, bf16[512,512]{1,0:T(8,128)(2,1)S(1)}, u32[]{:S(2)}, u32[]{:S(2)}) collective-permute-start(bf16[512,512]{1,0:T(8,128)(2,1)S(1)} %fusion.16), channel_id=1, source_target_pairs={{0,4},{4,8},{8,12},{12,16},{16,20},{20,24},{24,28},{28,0},{1,5},{5... | collective-permute-start | bytes 1572872 | tf_op jit(solution)/shard_map/ppermute | solution.py:16
Sparse Core Ops, SparseCore 0:
  10.4 29.3 all-gather.2
  43.8 24.7 reduce-scatter.2
  70.6 26.6 all-gather.4
  101.3 24.7 reduce-scatter.4
where the time goes:
time: 174 us; the launch traced here: 173 us
  waiting for transfers between devices  105 us (60%)
  matrix products  20.5 us (12%)
  blocking collectives  20 us (11%)
  between operations  13.8 us (8%)
  other arithmetic  7.74 us (4%)
  local copies, waits for them, and re-layouts  4.36 us (3%)
  starting transfers between devices  1.82 us (1%)
    reduce_scatter x2, waiting for transfers between devices, per_device(): lax.psum_scatter((jnp.dot(hidden_b, bf_b, preferred_element_type=jnp.floa...  46.4 us
    all_gather x2, waiting for transfers between devices, per_device(): all_rows = lax.all_gather(local_rows, 'batch', axis=0, tiled=True)  40.2 us
    all_gather x2, blocking collectives, per_device(): lax.all_gather((precision_obs * own_errors).astype(jnp.bfloat16), 'batch'...  20 us
    ppermute x2, waiting for transfers between devices, passed_along(): lax.ppermute(value, axis, [(i, (i + by) % size) for i in range(size)])  18.6 us
    dot_general x2, matrix products, per_device(): lax.dot_general(all_rows, back_hidden, contract_rows, preferred_element_t...  9.51 us
    dot_general x2, matrix products, per_device(): jnp.dot(all_rows, bf_a, preferred_element_type=jnp.float32) * scale_in  5.27 us
    broadcast_in_dim x3, other arithmetic, per_device(): return (moved_a[None], moved_b[None], own_errors.astype(jnp.bfloat16)[None])  4.4 us
  transfers between devices with their start and end apart: 6, of which 5 were waited for; matrix products, arithmetic and copies ran while one was open for 8% of the time, Pallas kernels for 0%

commit v1 on v0

--- a/solution.py
+++ b/solution.py
@@ -9,6 +9,12 @@
 half_step = 0.01
 root_step = 0.02**0.5
 precision_obs = 32.0
+
+
+def in_order(blocks, dim):
+    blocks = jnp.moveaxis(blocks, 0, dim)
+    dims = blocks.shape
+    return blocks.reshape(*dims[:dim], dims[dim] * dims[dim + 1], *dims[dim + 2 :])
 
 
 def passed_along(value, axis, by):
@@ -30,7 +36,19 @@
         local_targets = jnp.take(data_targets[0], chosen, axis=0)
         bf_a = weights_a.astype(jnp.bfloat16)
         bf_b = weights_b.astype(jnp.bfloat16)
-        all_rows = lax.all_gather(local_rows, "batch", axis=0, tiled=True)
+        peers = lax.axis_size("batch")
+        pairs = [(i_2, (i_2 + 1) % peers) for i_2 in range(peers)]
+        back = [(b, a) for a, b in pairs]
+        lower, upper = ([], [])
+        for step in range(peers - 1):
+            if step % 2 == 0:
+                lower.append(lax.ppermute(lower[-1] if lower else local_rows, "batch", pairs))
+            else:
+                upper.append(lax.ppermute(upper[-1] if upper else local_rows, "batch", back))
+        parts = jnp.stack([*lower[::-1], local_rows, *upper])
+        shift = lax.axis_index("batch") - len(lower)
+        parts = parts[(jnp.arange(peers) - shift) % peers]
+        all_rows = in_order(parts, 0)
         hidden = jnp.tanh(jnp.dot(all_rows, bf_a, preferred_element_type=jnp.float32) * scale_in)
         hidden_b = hidden.astype(jnp.bfloat16)
         predicted = lax.psum_scatter(

time: 174 us -> 161 us (0.925)
  waiting for transfers between devices: 105 us -> 78.1 us
  starting transfers between devices: 1.82 us -> 9.78 us
  other arithmetic: 7.74 us -> 11.5 us
  local copies, waits for them, and re-layouts: 4.36 us -> 7.94 us
  matrix products: 20.5 us -> 18.3 us
    all_gather x2 -> x0, waiting for transfers between devices: 40.2 us -> none  [per_device(): all_rows = lax.all_gather(local_rows, 'batch', axis=0, tiled=True)]
    ppermute x0 -> x6, waiting for transfers between devices: none -> 35.3 us  [the longest x4 26.3 us: per_device(): lax.ppermute(lower[-1] if lower else local_rows, 'batch', pairs)]
    reduce_scatter x2, waiting for transfers between devices: 46.4 us -> 24.4 us  [per_device(): lax.psum_scatter((jnp.dot(hidden_b, bf_b, preferred_element_type=jnp.floa...]
    ppermute x0 -> x6, starting transfers between devices: none -> 8.04 us  [the longest x4 4.88 us: per_device(): lax.ppermute(lower[-1] if lower else local_rows, 'batch', pairs)]
    another operation x0 -> x4, other arithmetic: none -> 3.48 us  [per_device(): parts = jnp.stack([*lower[::-1], local_rows, *upper])]
    gather x0 -> x2, local copies, waits for them, and re-layouts: none -> 3.42 us  [per_device(): parts = parts[(jnp.arange(peers) - shift) % peers]]
    dot_general x2, matrix products: 5.27 us -> 3.11 us  [per_device(): jnp.dot(all_rows, bf_a, preferred_element_type=jnp.float32) * scale_in]
  transfers between devices with their start and end apart: 6 -> 10, of which waited for: 5 -> 8; matrix products, arithmetic and copies ran while one was open for 8% -> 9% of each run, Pallas kernels for 0% -> 0%
where the time goes in v1:
time: 161 us
  waiting for transfers between devices  78.1 us (49%)
  blocking collectives  21.5 us (13%)
  matrix products  18.3 us (11%)
  between operations  14.2 us (9%)
  other arithmetic  11.5 us (7%)
  starting transfers between devices  9.78 us (6%)
  local copies, waits for them, and re-layouts  7.94 us (5%)
    ppermute x4, waiting for transfers between devices, per_device(): lax.ppermute(lower[-1] if lower else local_rows, 'batch', pairs)  26.3 us
    reduce_scatter x2, waiting for transfers between devices, per_device(): lax.psum_scatter((jnp.dot(hidden_b, bf_b, preferred_element_type=jnp.floa...  24.4 us
    all_gather x2, blocking collectives, per_device(): lax.all_gather((precision_obs * own_errors).astype(jnp.bfloat16), 'batch'...  21.5 us
    ppermute x2, waiting for transfers between devices, passed_along(): lax.ppermute(value, axis, [(i, (i + by) % size) for i in range(size)])  18.4 us
    dot_general x2, matrix products, per_device(): lax.dot_general(all_rows, back_hidden, contract_rows, preferred_element_t...  8.98 us
    ppermute x2, waiting for transfers between devices, per_device(): lax.ppermute(upper[-1] if upper else local_rows, 'batch', back)  8.94 us
    ppermute x4, starting transfers between devices, per_device(): lax.ppermute(lower[-1] if lower else local_rows, 'batch', pairs)  4.88 us
    broadcast_in_dim x3, other arithmetic, per_device(): return (moved_a[None], moved_b[None], own_errors.astype(jnp.bfloat16)[None])  4.4 us
  transfers between devices with their start and end apart: 10, of which 8 were waited for; matrix products, arithmetic and copies ran while one was open for 9% of the time, Pallas kernels for 0%

profile of v1, /device:TPU:0, one launch (start us, length us, event | category | flops | bytes accessed | tf_op | source)
XLA Modules:
  0.0 161.1 jit_solution(6257982826045063101)
XLA Ops:
  7.2 0.0 copy-start
  7.2 0.0 reduce-scatter.3.cloned.1.call-start
  7.2 0.7 compare_and_fusion
  7.9 0.1 copy-done
  8.1 0.9 gather_fusion.2
  8.9 0.1 broadcast_select_fusion.1
  9.0 3.0 %collective-permute-start = (bf16[128,1024]{1,0:T(8,128)(2,1)S(1)}, bf16[128,1024]{1,0:T(8,128)(2,1)S(1)}, u32[]{:S(2)}, u32[]{:S(2)}) collective-permute-start(bf16[128,1024]{1,0:T(8,128)(2,1)S(1)} %broadcast_select_fusion.1), channel_id=1, source_target_pairs={{0,1},{1,2},{2,3},{3,0},{4,5},{5,6},{6,7},{7,4},{8,9},{9,10},{10,1... | collective-permute-start | bytes 786440 | tf_op jit(solution)/shard_map/ppermute | solution.py:45
  12.0 1.0 collective-permute-start.2
  13.1 7.1 %collective-permute-done = bf16[128,1024]{1,0:T(8,128)(2,1)S(1)} collective-permute-done((bf16[128,1024]{1,0:T(8,128)(2,1)S(1)}, bf16[128,1024]{1,0:T(8,128)(2,1)S(1)}, u32[]{:S(2)}, u32[]{:S(2)}) %collective-permute-start) | collective-permute-done | bytes 262176 | tf_op jit(solution)/shard_map/ppermute | solution.py:45
  20.1 1.1 collective-permute-start.1
  21.2 0.1 fusion.61
  21.3 5.0 %collective-permute-done.2 = bf16[128,1024]{1,0:T(8,128)(2,1)S(1)} collective-permute-done((bf16[128,1024]{1,0:T(8,128)(2,1)S(1)}, bf16[128,1024]{1,0:T(8,128)(2,1)S(1)}, u32[]{:S(2)}, u32[]{:S(2)}) %collective-permute-start.2) | collective-permute-done | bytes 262176 | tf_op jit(solution)/shard_map/ppermute | solution.py:47
  26.3 4.2 %collective-permute-done.1 = bf16[128,1024]{1,0:T(8,128)(2,1)S(1)} collective-permute-done((bf16[128,1024]{1,0:T(8,128)(2,1)S(1)}, bf16[128,1024]{1,0:T(8,128)(2,1)S(1)}, u32[]{:S(2)}, u32[]{:S(2)}) %collective-permute-start.1) | collective-permute-done | bytes 262176 | tf_op jit(solution)/shard_map/ppermute | solution.py:45
  30.5 0.1 pad_maximum_fusion
  30.7 0.6 gather_fusion
  31.3 0.0 copy-start.2
  31.3 2.4 %fusion.13 = f32[512,512]{1,0:T(8,128)S(1)} fusion(bf16[512,1024]{1,0:T(8,128)(2,1)S(1)} %bitcast.79, f32[1,1024,512]{2,1,0:T(8,128)} %param.14), kind=kOutput, calls=%fused_computation.31 | convolution fusion | flops 537657344 | bytes 4194304 | tf_op jit(solution)/shard_map/dot_general | solution.py:52
  33.7 0.0 copy-done.2
  33.7 1.2 fusion.17
  34.9 0.0 copy-start.1
  34.9 0.0 reduce-scatter.3.cloned.1.call-update
  35.0 0.0 reduce-scatter.5.cloned.1.call-start
  35.0 1.6 gather_fusion.4
  36.6 1.7 %broadcast_select_fusion = bf16[128,1024]{1,0:T(8,128)(2,1)} fusion(bf16[128,1024]{1,0:T(8,128)(2,1)} %gather_fusion.4, pred[128]{0:T(512)(128)(4,1)S(1)} %get-tuple-element.5), kind=kLoop, calls=%fused_computation.62 | loop fusion | flops 131072 | bytes 524416 | tf_op jit(solution)/shard_map/jit(_take)/select_n | solution.py:35
  38.3 0.8 collective-permute-start.3
  39.1 2.1 %collective-permute-start.5 = (bf16[128,1024]{1,0:T(8,128)(2,1)}, bf16[128,1024]{1,0:T(8,128)(2,1)}, u32[]{:S(2)}, u32[]{:S(2)}) collective-permute-start(bf16[128,1024]{1,0:T(8,128)(2,1)} %broadcast_select_fusion), channel_id=1, source_target_pairs={{1,0},{2,1},{3,2},{0,3},{5,4},{6,5},{7,6},{4,7},{9,8},{10,9},{11,1... | collective-permute-start | bytes 786440 | tf_op jit(solution)/shard_map/ppermute | solution.py:47
  41.3 10.3 %collective-permute-done.3 = bf16[128,1024]{1,0:T(8,128)(2,1)} collective-permute-done((bf16[128,1024]{1,0:T(8,128)(2,1)}, bf16[128,1024]{1,0:T(8,128)(2,1)}, u32[]{:S(2)}, u32[]{:S(2)}) %collective-permute-start.3) | collective-permute-done | bytes 262176 | tf_op jit(solution)/shard_map/ppermute | solution.py:45
  51.6 0.0 collective-permute-start.4
  51.6 0.0 copy-done.1
  51.6 0.8 gather_fusion.3
  52.5 1.0 fusion.60
  53.5 4.0 %collective-permute-done.5 = bf16[128,1024]{1,0:T(8,128)(2,1)} collective-permute-done((bf16[128,1024]{1,0:T(8,128)(2,1)}, bf16[128,1024]{1,0:T(8,128)(2,1)}, u32[]{:S(2)}, u32[]{:S(2)}) %collective-permute-start.5) | collective-permute-done | bytes 262176 | tf_op jit(solution)/shard_map/ppermute | solution.py:47
  57.5 4.7 %collective-permute-done.4 = bf16[128,1024]{1,0:T(8,128)(2,1)} collective-permute-done((bf16[128,1024]{1,0:T(8,128)(2,1)}, bf16[128,1024]{1,0:T(8,128)(2,1)}, u32[]{:S(2)}, u32[]{:S(2)}) %collective-permute-start.4) | collective-permute-done | bytes 262176 | tf_op jit(solution)/shard_map/ppermute | solution.py:45
  62.2 2.2 %pad_maximum_fusion.1 = bf16[4,128,1024]{2,1,0:T(8,128)(2,1)} fusion(bf16[1,128,1024]{2,1,0:T(8,128)(2,1)} %bitcast.17, bf16[1,128,1024]{2,1,0:T(8,128)(2,1)S(1)} %fusion.60, bf16[1,128,1024]{2,1,0:T(8,128)(2,1)} %bitcast.15, bf16[1,128,1024]{2,1,0:T(8,128)(2,1)} %bitcast.14), kind=kLoop, calls=%fused_computation.38 | loop fusion | flops 1572864 | bytes 2097152 | tf_op jit(solution)/shard_map/stack | solution.py:48
  64.4 2.8 %gather_fusion.1 = bf16[4,128,1024]{2,1,0:T(8,128)(2,1)} fusion(bf16[4,128,1024]{2,1,0:T(8,128)(2,1)} %pad_maximum_fusion.1, s32[1024]{0:T(1024)S(1)} %pad_clamp_fusion.1), kind=kCustom, calls=%fused_computation.5 | custom fusion | bytes 2097168 | tf_op jit(solution)/shard_map/gather | solution.py:50
  67.2 0.0 reduce-scatter.3.cloned.1.call-done
  67.2 1.0 multiply_convert_fusion.1
  68.2 10.9 %all_gather.6 = bf16[512,512]{1,0:T(8,128)(2,1)} all-gather(bf16[128,512]{1,0:T(8,128)(2,1)S(1)} %multiply_convert_fusion.1), channel_id=1, replica_groups=mesh['shard'=8,'batch'=4] {'batch'}, dimensions={0}, use_global_device_ids=true | all-gather | bytes 655360 | tf_op jit(solution)/shard_map/all_gather | solution.py:63
  79.1 4.6 %bitcast_add_fusion.1 = f32[1024,512]{1,0:T(8,128)} fusion(f32[1,1024,512]{2,1,0:T(8,128)} %param.14, bf16[512,1024]{1,0:T(8,128)(2,1)S(1)} %bitcast.80, bf16[512,512]{1,0:T(8,128)(2,1)} %all_gather.6, bf16[2,1,1024,512]{3,2,1,0:T(8,128)(2,1)} %param.16, f32[512,512]{1,0:T(8,128)S(1)} %fusion.13, f32[1,512,512]{2,1,0:T(8,128)S(1)} %copy-done.2), kind=kOutput, calls=%fused_computation.8 | convolution fusion | flops 810287104 | bytes 8912896 | tf_op jit(solution)/shard_map/dot_general | solution.py:76
  83.7 0.0 copy-start.3
  83.7 0.0 copy-start.4
  83.7 1.9 %fusion.10 = f32[512,512]{1,0:T(8,128)S(1)} fusion(bf16[512,512]{1,0:T(8,128)(2,1)} %all_gather.6, f32[1,512,512]{2,1,0:T(8,128)S(1)} %copy-done.2, bf16[2,1,512,512]{3,2,1,0:T(8,128)(2,1)} %param.17, f32[512,512]{1,0:T(8,128)S(1)} %fusion.13), kind=kOutput, calls=%fused_computation.24 | convolution fusion | flops 270532608 | bytes 4194304 | tf_op jit(solution)/shard_map/dot_general | solution.py:67
  85.7 0.0 copy-done.3
  85.7 0.2 copy-done.4
  85.9 0.7 fusion.11
  86.6 1.2 fusion.18
  87.9 0.0 copy-start.5
  87.9 0.0 reduce-scatter.5.cloned.1.call-update
  87.9 0.8 gather_fusion.5
  88.8 24.4 %reduce-scatter.5.cloned.1.call-done = bf16[128,512]{1,0:T(8,128)(2,1)} async-done(((bf16[512,512]{1,0:T(8,128)(2,1)}), bf16[128,512]{1,0:T(8,128)(2,1)}) %reduce-scatter.5.cloned.1.call-update) | async-done | bytes 131088 | tf_op jit(solution)/shard_map/reduce_scatter | solution.py:54
  113.1 1.7 %fusion.38 = (bf16[1,128,512]{2,1,0:T(8,128)(2,1)}, bf16[128,512]{1,0:T(8,128)(2,1)S(1)}) fusion(bf16[128,512]{1,0:T(8,128)(2,1)} %reduce-scatter.5.cloned.1.call-done, bf16[128,512]{1,0:T(8,128)(2,1)S(1)} %gather_fusion.5, pred[128]{0:T(512)(128)(4,1)S(1)} %get-tuple-element.5), kind=kLoop, calls=%fused_computation.65 | loop fusion | flops 458752 | bytes 524416 | tf_op jit(solution)/shard_map/broadcast_in_dim | solution.py:95
  114.8 10.6 %all_gather.7 = bf16[512,512]{1,0:T(8,128)(2,1)} all-gather(bf16[128,512]{1,0:T(8,128)(2,1)S(1)} %get-tuple-element.10), channel_id=1, replica_groups=mesh['shard'=8,'batch'=4] {'batch'}, dimensions={0}, use_global_device_ids=true | all-gather | bytes 655360 | tf_op jit(solution)/shard_map/all_gather | solution.py:63
  125.4 0.0 copy-done.5
  125.4 4.3 %fusion = bf16[1024,512]{1,0:T(8,128)(2,1)} fusion(f32[1024,512]{1,0:T(8,128)} %bitcast_add_fusion.1, bf16[512,1024]{1,0:T(8,128)(2,1)S(1)} %bitcast.82, bf16[512,512]{1,0:T(8,128)(2,1)} %all_gather.7, bf16[2,1,1024,512]{3,2,1,0:T(8,128)(2,1)} %param.16, f32[512,512]{1,0:T(8,128)S(1)} %fusion.11, f32[512,512]{1,0:T(8,128)S(1)} %fusion.10), kind=kOutput, calls=%fused_computation.7 | convolution fusion | flops 811073536 | bytes 7864320 | tf_op jit(solution)/shard_map/dot_general | solution.py:76
  129.7 0.0 collective-permute-start.6
  129.7 1.8 %fusion.16 = bf16[512,512]{1,0:T(8,128)(2,1)S(1)} fusion(f32[512,512]{1,0:T(8,128)S(1)} %fusion.10, bf16[512,512]{1,0:T(8,128)(2,1)} %all_gather.7, bf16[2,1,512,512]{3,2,1,0:T(8,128)(2,1)} %param.17, f32[512,512]{1,0:T(8,128)S(1)} %fusion.11), kind=kOutput, calls=%fused_computation.34 | convolution fusion | flops 270794752 | bytes 3670016 | tf_op jit(solution)/shard_map/dot_general | solution.py:67
  131.5 1.7 %collective-permute-start.7 = (bf16[512,512]{1,0:T(8,128)(2,1)S(1)}, bf16[512,512]{1,0:T(8,128)(2,1)S(1)}, u32[]{:S(2)}, u32[]{:S(2)}) collective-permute-start(bf16[512,512]{1,0:T(8,128)(2,1)S(1)} %fusion.16), channel_id=1, source_target_pairs={{0,4},{4,8},{8,12},{12,16},{16,20},{20,24},{24,28},{28,0},{1,5},{5... | collective-permute-start | bytes 1572872 | tf_op jit(solution)/shard_map/ppermute | solution.py:22
  133.2 18.4 %collective-permute-done.7 = bf16[512,512]{1,0:T(8,128)(2,1)S(1)} collective-permute-done((bf16[512,512]{1,0:T(8,128)(2,1)S(1)}, bf16[512,512]{1,0:T(8,128)(2,1)S(1)}, u32[]{:S(2)}, u32[]{:S(2)}) %collective-permute-start.7) | collective-permute-done | bytes 524320 | tf_op jit(solution)/shard_map/ppermute | solution.py:22
  151.6 1.1 bitcast_convert_fusion.2
  152.7 0.0 collective-permute-done.6
  152.7 1.6 %bitcast_convert_fusion = f32[1,1024,512]{2,1,0:T(8,128)} fusion(bf16[1024,512]{1,0:T(8,128)(2,1)S(1)} %collective-permute-done.6), kind=kLoop, calls=%fused_computation.39 | loop fusion | flops 524288 | bytes 3145728 | tf_op jit(solution)/shard_map/broadcast_in_dim | solution.py:95
  (4 shorter events, 0.0 us)
Async XLA Ops:
  7.2 0.9 copy-start
  7.2 60.0 %reduce-scatter.3.cloned.1.call-start = ((), (), s32[]{:S(2)}) async-start(), calls=%async_computation.2 | async-start | bytes 655360 | tf_op jit(solution)/shard_map/reduce_scatter | solution.py:54
  9.0 11.1 %collective-permute-start = (bf16[128,1024]{1,0:T(8,128)(2,1)S(1)}, bf16[128,1024]{1,0:T(8,128)(2,1)S(1)}, u32[]{:S(2)}, u32[]{:S(2)}) collective-permute-start(bf16[128,1024]{1,0:T(8,128)(2,1)S(1)} %broadcast_select_fusion.1), channel_id=1, source_target_pairs={{0,1},{1,2},{2,3},{3,0},{4,5},{5,6},{6,7},{7,4},{8,9},{9,10},{10,1... | collective-permute-start | bytes 786440 | tf_op jit(solution)/shard_map/ppermute | solution.py:45
  12.0 14.3 %collective-permute-start.2 = (bf16[128,1024]{1,0:T(8,128)(2,1)S(1)}, bf16[128,1024]{1,0:T(8,128)(2,1)S(1)}, u32[]{:S(2)}, u32[]{:S(2)}) collective-permute-start(bf16[128,1024]{1,0:T(8,128)(2,1)S(1)} %broadcast_select_fusion.1), channel_id=1, source_target_pairs={{1,0},{2,1},{3,2},{0,3},{5,4},{6,5},{7,6},{4,7},{9,8},{10,9},{11,1... | collective-permute-start | bytes 786440 | tf_op jit(solution)/shard_map/ppermute | solution.py:47
  20.1 10.4 %collective-permute-start.1 = (bf16[128,1024]{1,0:T(8,128)(2,1)S(1)}, bf16[128,1024]{1,0:T(8,128)(2,1)S(1)}, u32[]{:S(2)}, u32[]{:S(2)}) collective-permute-start(bf16[128,1024]{1,0:T(8,128)(2,1)S(1)} %collective-permute-done), channel_id=1, source_target_pairs={{0,1},{1,2},{2,3},{3,0},{4,5},{5,6},{6,7},{7,4},{8,9},{9,10},{10,1... | collective-permute-start | bytes 786440 | tf_op jit(solution)/shard_map/ppermute | solution.py:45
  31.3 2.4 %copy-start.2 = (f32[1,512,512]{2,1,0:T(8,128)S(1)}, f32[1,512,512]{2,1,0:T(8,128)}, u32[]{:S(2)}) copy-start(f32[1,512,512]{2,1,0:T(8,128)} %param.15) | copy-start | bytes 3145732
  34.9 16.7 %copy-start.1 = (bf16[1,64,512]{2,1,0:T(8,128)(2,1)S(1)}, bf16[1,64,512]{2,1,0:T(8,128)(2,1)}, u32[]{:S(2)}) copy-start(bf16[1,64,512]{2,1,0:T(8,128)(2,1)} %param.12) | copy-start | bytes 196612
  35.0 78.1 %reduce-scatter.5.cloned.1.call-start = ((), (), s32[]{:S(2)}) async-start(), calls=%async_computation.3 | async-start | bytes 655360 | tf_op jit(solution)/shard_map/reduce_scatter | solution.py:54
  38.3 13.3 %collective-permute-start.3 = (bf16[128,1024]{1,0:T(8,128)(2,1)}, bf16[128,1024]{1,0:T(8,128)(2,1)}, u32[]{:S(2)}, u32[]{:S(2)}) collective-permute-start(bf16[128,1024]{1,0:T(8,128)(2,1)} %broadcast_select_fusion), channel_id=1, source_target_pairs={{0,1},{1,2},{2,3},{3,0},{4,5},{5,6},{6,7},{7,4},{8,9},{9,10},{10,1... | collective-permute-start | bytes 786440 | tf_op jit(solution)/shard_map/ppermute | solution.py:45
  39.1 18.3 %collective-permute-start.5 = (bf16[128,1024]{1,0:T(8,128)(2,1)}, bf16[128,1024]{1,0:T(8,128)(2,1)}, u32[]{:S(2)}, u32[]{:S(2)}) collective-permute-start(bf16[128,1024]{1,0:T(8,128)(2,1)} %broadcast_select_fusion), channel_id=1, source_target_pairs={{1,0},{2,1},{3,2},{0,3},{5,4},{6,5},{7,6},{4,7},{9,8},{10,9},{11,1... | collective-permute-start | bytes 786440 | tf_op jit(solution)/shard_map/ppermute | solution.py:47
  51.6 10.6 %collective-permute-start.4 = (bf16[128,1024]{1,0:T(8,128)(2,1)}, bf16[128,1024]{1,0:T(8,128)(2,1)}, u32[]{:S(2)}, u32[]{:S(2)}) collective-permute-start(bf16[128,1024]{1,0:T(8,128)(2,1)} %collective-permute-done.3), channel_id=1, source_target_pairs={{0,1},{1,2},{2,3},{3,0},{4,5},{5,6},{6,7},{7,4},{8,9},{9,10},{10,1... | collective-permute-start | bytes 786440 | tf_op jit(solution)/shard_map/ppermute | solution.py:45
  83.7 1.9 %copy-start.3 = (f32[1024,512]{1,0:T(8,128)S(1)}, f32[1024,512]{1,0:T(8,128)}, u32[]{:S(2)}) copy-start(f32[1024,512]{1,0:T(8,128)} %bitcast_add_fusion.1) | copy-start | bytes 6291460
  83.7 2.2 %copy-start.4 = (bf16[4,128,1024]{2,1,0:T(8,128)(2,1)S(1)}, bf16[4,128,1024]{2,1,0:T(8,128)(2,1)}, u32[]{:S(2)}) copy-start(bf16[4,128,1024]{2,1,0:T(8,128)(2,1)} %gather_fusion.1) | copy-start | bytes 3145732
  87.9 37.5 %copy-start.5 = (bf16[4,128,1024]{2,1,0:T(8,128)(2,1)S(1)}, bf16[4,128,1024]{2,1,0:T(8,128)(2,1)}, u32[]{:S(2)}) copy-start(bf16[4,128,1024]{2,1,0:T(8,128)(2,1)} %gather_fusion.1) | copy-start | bytes 3145732
  129.7 23.0 %collective-permute-start.6 = (bf16[1024,512]{1,0:T(8,128)(2,1)}, bf16[1024,512]{1,0:T(8,128)(2,1)S(1)}, u32[]{:S(2)}, u32[]{:S(2)}) collective-permute-start(bf16[1024,512]{1,0:T(8,128)(2,1)} %fusion), channel_id=1, source_target_pairs={{0,4},{4,8},{8,12},{12,16},{16,20},{20,24},{24,28},{28,0},{1,5},{5... | collective-permute-start | bytes 3145736 | tf_op jit(solution)/shard_map/ppermute | solution.py:22
  131.5 20.1 %collective-permute-start.7 = (bf16[512,512]{1,0:T(8,128)(2,1)S(1)}, bf16[512,512]{1,0:T(8,128)(2,1)S(1)}, u32[]{:S(2)}, u32[]{:S(2)}) collective-permute-start(bf16[512,512]{1,0:T(8,128)(2,1)S(1)} %fusion.16), channel_id=1, source_target_pairs={{0,4},{4,8},{8,12},{12,16},{16,20},{20,24},{24,28},{28,0},{1,5},{5... | collective-permute-start | bytes 1572872 | tf_op jit(solution)/shard_map/ppermute | solution.py:22
Sparse Core Ops, SparseCore 0:
  35.1 28.2 reduce-scatter.2
  88.0 25.0 reduce-scatter.4
